TPU v7x, 32 devices: a whole 2x2x4 slice. The times are simulated.
32 devices in a mesh: ctx: 8 (over z, x), fsdp: 4 (over y, core).
Axes of the slice: x: 2, y: 2, z: 4, core: 2. Of those that a mesh axis runs over, the one named last changes fastest.
Arguments:
- inputs: bfloat16 [8, 512, 768], P('fsdp', 'ctx'), may hold values from -6 to 6
- w_qkv: bfloat16 [2, 3, 768, 768], P(None, None, ('ctx', 'fsdp')), may hold values from -0.21650635 to 0.21650635
- w_out: bfloat16 [2, 768, 768], P(None, ('ctx', 'fsdp')), may hold values from -4.8989795 to 4.8989795
- w_up: bfloat16 [2, 768, 3072], P(None, ('ctx', 'fsdp')), may hold values from -0.21875 to 0.21875
- w_down: bfloat16 [2, 3072, 768], P(None, ('ctx', 'fsdp')), may hold values from -0.109375 to 0.109375
- biases: bfloat16 [2, 3, 768], P(None, None, ('ctx', 'fsdp')), may hold values from -1.75 to 1.75
- value_bias: bfloat16 [2, 768], P(None, ('ctx', 'fsdp')), may hold values from -0.078125 to 0.078125
- up_bias: bfloat16 [2, 3072], P(None, ('ctx', 'fsdp')), may hold values from -1.75 to 1.75
- gains: bfloat16 [2, 2, 768], P(None, None, ('ctx', 'fsdp')), may hold values from 0.5 to 1.5
- shifts: bfloat16 [2, 2, 768], P(None, None, ('ctx', 'fsdp')), may hold values from -1.75 to 1.75
- cotangent: bfloat16 [8, 512, 768], P('fsdp', 'ctx'), may hold values from -8 to 8
Outputs:
- output: bfloat16 [8, 512, 768], P('fsdp', 'ctx')
- grad_inputs: bfloat16 [8, 512, 768], P('fsdp', 'ctx')
- grad_w_qkv: float32 [2, 3, 768, 768], P(None, None, ('ctx', 'fsdp'))
- grad_w_out: float32 [2, 768, 768], P(None, ('ctx', 'fsdp'))
- grad_w_up: float32 [2, 768, 3072], P(None, ('ctx', 'fsdp'))
- grad_w_down: float32 [2, 3072, 768], P(None, ('ctx', 'fsdp'))
- grad_biases: float32 [2, 3, 768], P(None, None, ('ctx', 'fsdp'))
- grad_value_bias: float32 [2, 768], P(None, ('ctx', 'fsdp'))
- grad_up_bias: float32 [2, 3072], P(None, ('ctx', 'fsdp'))
- grad_gains: float32 [2, 2, 768], P(None, None, ('ctx', 'fsdp'))
- grad_shifts: float32 [2, 2, 768], P(None, None, ('ctx', 'fsdp'))
All inputs are finite; a program needn't handle non-finite values.
Results may differ from a plain program's by a relative error of at most 0.024.
Values may be sent and summed in bfloat16 or wider, within the bound.
A program may use at most 320 MiB of HBM per device.

v0:
```python
import functools
import types

import jax
import jax.numpy as jnp
from jax import lax
from jax.experimental import pallas as pl
from jax.experimental.pallas import tpu as pltpu
from jax.sharding import PartitionSpec as P

D = 768
HEADS = 12
HEAD_DIM = 64
LAYERS = 2
KERNEL_VMEM = 63 * 2**20


BF = jnp.bfloat16
F32 = jnp.float32
MESH = pl.DeviceIdType.MESH
MEMBERS = 4
LOCAL_HEADS = HEADS // MEMBERS
PACK = 640
SLOT = 64
PIECE = 64


def dot_nn(left, right):
    return lax.dot_general(left, right, (((1,), (0,)), ((), ())), preferred_element_type=F32)


def dot_nt(left, right):
    return lax.dot_general(left, right, (((1,), (1,)), ((), ())), preferred_element_type=F32)


def dot_tn(left, right):
    return lax.dot_general(left, right, (((0,), (0,)), ((), ())), preferred_element_type=F32)


def dot_exact(left, right):
    return lax.dot_general(
        left,
        right,
        (((1,), (0,)), ((), ())),
        precision=lax.Precision.HIGHEST,
        preferred_element_type=F32,
    )


def packed_lanes(shape, axis):
    lane = lax.broadcasted_iota(jnp.int32, shape, axis)
    slot = lane >> 6
    head = jnp.where(slot >= 6, 2, slot & 1)
    is_query = (slot < 2) | (slot == 6)
    is_value = (slot == 4) | (slot == 5) | (slot == 8)
    return (head * HEAD_DIM + (lane & 63), is_query, is_value)


def scratch_layout(nz, ny, rows, half, d_rows, f_rows):
    dma = pltpu.SemaphoreType.DMA
    two = 2 * d_rows
    ff = nz * ny * f_rows
    vm = pltpu.VMEM
    return dict(
        wq=vm((LAYERS, nz, 2, ny, two, PACK), BF),
        wu=vm((LAYERS, nz, 2, ny, two, ff), BF),
        wd=vm((LAYERS, nz, ny, f_rows, D), BF),
        wog=vm((nz, ny, two, D), BF),
        wo=vm((LAYERS, 256, D), BF),
        smg=vm((nz, ny, MEMBERS, 32, 128), BF),
        qi=vm((MEMBERS, two, PACK), BF),
        ui=vm((MEMBERS, two, ff), BF),
        oi=vm((two, D), BF),
        sf=vm((32, 128), F32),
        si=vm((32, 128), BF),
        qs=vm((MEMBERS, two, PACK), BF),
        us=vm((MEMBERS, two, ff), BF),
        pb=vm((16, D), F32),
        ub=vm((16, ff), F32),
        bq=vm((LAYERS, 8, PACK), F32),
        xf=vm((LAYERS, rows, D), BF),
        qkv=vm((LAYERS, rows, PACK), BF),
        prob=vm((LAYERS, LOCAL_HEADS, rows, rows), BF),
        mix=vm((LAYERS, rows, 256), F32),
        mixl=vm((LAYERS, rows, 256), BF),
        xh1=vm((LAYERS, half, D), F32),
        iv1=vm((LAYERS, half, 128), F32),
        nl=vm((LAYERS, rows, D), BF),
        gp=vm((LAYERS, rows, ff), F32),
        act=vm((LAYERS, rows, ff), BF),
        xh2=vm((LAYERS, half, D), F32),
        iv2=vm((LAYERS, half, 128), F32),
        stream=vm((half, D), F32),
        normed=vm((half, D), F32),
        ct=vm((half, D), BF),
        ownp=vm((half, D), F32),
        sibs=vm((2, half, D), BF),
        sibr=vm((2, half, D), BF),
        xs=vm((2, half, D), BF),
        xr=vm((2, half, D), BF),
        dl=vm((rows, D), BF),
        db=vm((rows, D), BF),
        du=vm((rows, ff), BF),
        dq=vm((rows, PACK), BF),
        dm=vm((rows, 256), BF),
        ds=vm((LOCAL_HEADS, rows, rows), BF),
        back=vm((2, half, D), BF),
        land=vm((2, 2, rows // (2 * nz), D), BF),
        gq=vm((LAYERS, nz, 2, ny, two, PACK), BF),
        gu=vm((LAYERS, nz, 2, ny, two, ff), BF),
        gd=vm((LAYERS, nz, ny, f_rows, D), BF),
        go=vm((LAYERS, nz, ny, 32, D), BF),
        ryq=vm((LAYERS, nz, 2, two, PACK), BF),
        ryu=vm((LAYERS, nz, 2, two, ff), BF),
        ryd=vm((nz, f_rows, D), BF),
        ryl=vm((f_rows, D), BF),
        syl=vm((f_rows, D), BF),
        ryo=vm((LAYERS, nz, 32, D), BF),
        rzq=vm((LAYERS, 4, 2, two, PACK), BF),
        rzu=vm((LAYERS, 4, 2, two, ff), BF),
        rzd=vm((4, f_rows, D), BF),
        rzl=vm((4, 2, f_rows, D), BF),
        rzo=vm((LAYERS, 4, 32, D), BF),
        fq=vm((LAYERS, 2, two, PACK), F32),
        fu=vm((LAYERS, 2, two, ff), F32),
        fo=vm((LAYERS, d_rows, D), F32),
        oq=vm((LAYERS, MEMBERS, d_rows, PACK), F32),
        ou=vm((LAYERS, MEMBERS, d_rows, ff), F32),
        oo=vm((LAYERS, d_rows, D), F32),
        sg=vm((LAYERS, 8, D), F32),
        sgy=vm((LAYERS, 8, D), F32),
        sgt=vm((LAYERS, 8, D), F32),
        sgz=vm((LAYERS, nz, 8, D), F32),
        sga=vm((LAYERS, MEMBERS, 8, D), F32),
        stage_s=dma((3, 3)),
        stage_r=dma((3, 3)),
        perm=dma((2,)),
        in_s=dma((4, 2)),
        in_r=dma((4, 2)),
        inx_s=dma((2, 2)),
        inx_r=dma((2, 2)),
        ins_s=dma((1,)),
        ins_r=dma((1,)),
        gz_s=dma((8, nz)),
        gz_r=dma((8, nz)),
        gy_s=dma((8, nz)),
        gy_r=dma((8, nz)),
        sib_s=dma((2, half // PIECE)),
        sib_r=dma((2, half // PIECE)),
        x_s=dma((2, half // PIECE)),
        x_r=dma((2, half // PIECE)),
        ag_s=dma((2, half // PIECE)),
        ag_r=dma((2, half // PIECE)),
        ry_s=dma((8,)),
        ry_r=dma((8,)),
        rz_s=dma((8, nz)),
        rz_r=dma((8, nz)),
        fin_s=dma((LAYERS, 2, 3)),
        fin_r=dma((LAYERS, 2, 3)),
        fino=dma((LAYERS, 2)),
        sgy_s=dma((LAYERS,)),
        sgy_r=dma((LAYERS,)),
        sgz_s=dma((LAYERS, nz)),
        sgz_r=dma((LAYERS, nz)),
        sga_s=dma((LAYERS, 3)),
        sga_r=dma((LAYERS, 3)),
    )


def group_kernel(layout, nz, *refs):
    inp, w_qkv, w_out, w_up, d_in, biases, value_bias, up_bias, gains, shifts, cot = refs[:11]
    out, gin, g_qkv, o_out, g_up, d_out, g_biases, g_value, g_raise, g_gains, g_shifts = refs[11:22]
    S = types.SimpleNamespace(**dict(zip(layout.keys(), refs[22:])))
    q_in, u_in, o_in, s_in = S.qi, S.ui, S.oi, S.si
    rows = S.dl.shape[0]
    half = rows // 2
    block = inp.shape[1]
    d_rows = w_out.shape[1]
    f_rows = d_in.shape[1]
    two = 2 * d_rows
    ff = S.du.shape[1]
    pieces = half // PIECE
    place = lax.axis_index("ctx")
    lane_f = lax.axis_index("fsdp")
    z, x = lax.div(place, 2), lax.rem(place, 2)
    y, c = lax.div(lane_f, 2), lax.rem(lane_f, 2)
    m = 2 * x + c
    d = 4 * place + lane_f
    devices = 8 * nz

    def dev(z_at, x_at, y_at, c_at):
        return (2 * z_at + x_at, 2 * y_at + c_at)

    def rcopy(source, target, send, recv, to):
        return pltpu.make_async_remote_copy(
            src_ref=source,
            dst_ref=target,
            send_sem=send,
            recv_sem=recv,
            device_id=to,
            device_id_type=MESH,
        )

    barrier = pltpu.get_barrier_semaphore()

    def hail(step, carry):
        other = lax.rem(d + step, devices)
        pl.semaphore_signal(
            barrier, inc=1, device_id=(lax.div(other, 4), lax.rem(other, 4)), device_id_type=MESH
        )
        return carry

    lax.fori_loop(1, devices, hail, 0)

    lane_low = lax.broadcasted_iota(jnp.int32, (1, 128), 1) < HEAD_DIM

    def turn(value):
        return pltpu.roll(value, HEAD_DIM, 1)

    def pack_heads(layer, pair):
        tiles = []
        for kind in range(3):
            base = 2 * pair * LOCAL_HEADS * HEAD_DIM
            whole = w_qkv[layer, kind, :, base : base + 384].astype(F32)
            tiles.append([whole[:, 0:128], whole[:, 128:256], whole[:, 256:384]])
        (q0, q1, q2), (k0, k1, k2), (v0, v1, v2) = tiles
        even = (q0, k0, v0, jnp.where(lane_low, q1, turn(k1)), jnp.where(lane_low, v1, 0.0))
        odd = (
            jnp.where(lane_low, turn(q1), turn(q2)),
            jnp.where(lane_low, turn(k1), turn(k2)),
            jnp.where(lane_low, turn(v1), turn(v2)),
            jnp.where(lane_low, turn(q2), k2),
            jnp.where(lane_low, turn(v2), 0.0),
        )
        return [jnp.concatenate(part, axis=1) for part in (even, odd)]

    for pair in range(2):
        packed = [pack_heads(layer, pair) for layer in range(LAYERS)]
        for odd in range(2):
            both = jnp.concatenate([part[odd] for part in packed], axis=0)
            q_in[2 * pair + odd] = both.astype(BF)

    def owner_block(z_at, x_at, y_at, c_at):
        at = (8 * z_at + 4 * x_at + 2 * y_at + c_at) * f_rows
        return slice(at, at + f_rows)

    grid_places = [(z_at, y_at) for z_at in range(nz) for y_at in range(2)]

    def pack_raise():
        wide = [w_up[layer].astype(F32) for layer in range(LAYERS)]
        for x_at in range(2):
            for c_at in range(2):
                both = [
                    jnp.concatenate(
                        [part[:, owner_block(z_at, x_at, y_at, c_at)] for z_at, y_at in grid_places], axis=1
                    )
                    for part in wide
                ]
                u_in[2 * x_at + c_at] = jnp.concatenate(both, axis=0).astype(BF)

    def pack_small():
        S.sf[...] = jnp.zeros_like(S.sf)
        for layer in range(LAYERS):
            base = 8 * layer
            S.sf[base : base + 3, 0:d_rows] = biases[layer].astype(F32)
            S.sf[base + 3 : base + 4, 0:d_rows] = value_bias[layer : layer + 1].astype(F32)
            S.sf[base + 4 : base + 6, 0:d_rows] = gains[layer].astype(F32)
            S.sf[base + 6 : base + 8, 0:d_rows] = shifts[layer].astype(F32)
            S.sf[16 + layer : 17 + layer, 0:f_rows] = up_bias[layer : layer + 1].astype(F32)
        s_in[...] = S.sf[...].astype(BF)

    pack_small()
    pack_raise()
    o_in[...] = jnp.concatenate([w_out[layer].astype(F32) for layer in range(LAYERS)], axis=0).astype(BF)
    pl.semaphore_wait(barrier, devices - 1)

    relation = ((x, 1 - c), (1 - x, c), (1 - x, 1 - c))
    sibling = dev(z, x, y, 1 - c)
    peer = dev(z, 1 - x, y, c)
    across = dev(z, x, 1 - y, c)

    def stage_copy(kind, r):
        x_r, c_r = relation[r]
        m_r = 2 * x_r + c_r
        source = (s_in, q_in.at[m_r], u_in.at[m_r])[kind]
        target = (S.smg.at[z, y, m], S.qs.at[m], S.us.at[m])[kind]
        return rcopy(source, target, S.stage_s.at[kind, r], S.stage_r.at[kind, r], dev(z, x_r, y, c_r))

    def stage_wait(kind, r):
        x_r, c_r = relation[r]
        m_r = 2 * x_r + c_r
        target = (S.smg.at[z, y, m_r], S.qs.at[m_r], S.us.at[m_r])[kind]
        rcopy(
            target, target, S.stage_s.at[kind, r], S.stage_r.at[kind, r], dev(z, x_r, y, c_r)
        ).wait_recv()

    for kind in (1, 0):
        for r in (1, 2, 0):
            stage_copy(kind, r).start()

    def own_block(j):
        return (2 * c + j == z) & (lax.div(z, 2) == c)

    def scatter_in(which, source, target, position):
        for j in range(2):
            copy = rcopy(
                source.at[j],
                target.at[pl.ds(position, block)],
                S.in_s.at[which, j],
                S.in_r.at[which, lax.rem(z, 2)],
                dev(2 * c + j, x, y, lax.div(z, 2)),
            )

            @pl.when(own_block(j))
            def _():
                target[pl.ds(position, block), :] = source[j]

            @pl.when(jnp.logical_not(own_block(j)))
            def _():
                copy.start()

    def scatter_in_wait(which, source, target, base):
        for k in range(2):

            @pl.when(2 * c + k != z)
            def _():
                spot = target.at[pl.ds(base + 2 * block * k, block)]
                rcopy(
                    spot, spot, S.in_s.at[which, 0], S.in_r.at[which, k], peer
                ).wait_recv()

    def scatter_in_drain(which, source, target):
        for j in range(2):

            @pl.when(jnp.logical_not(own_block(j)))
            def _():
                rcopy(
                    source.at[j], source.at[j], S.in_s.at[which, j], S.in_r.at[which, 0], peer
                ).wait_send()

    first = S.xf.at[0]
    scatter_in(0, inp, first, block * place)

    perm_to = dev(2 * x + y, lax.div(z, 2), c, lax.rem(z, 2))
    perm_stays = (2 * x + y == z) & (lax.div(z, 2) == x) & (c == y) & (lax.rem(z, 2) == c)
    perm_copy = rcopy(o_in, S.wog.at[2 * x + y, c], S.perm.at[0], S.perm.at[1], perm_to)

    @pl.when(perm_stays)
    def _():
        S.wog[z, y] = o_in[...]

    def start_perm():
        @pl.when(jnp.logical_not(perm_stays))
        def _():
            perm_copy.start()

    start_perm()
    for r in (1, 2, 0):
        stage_copy(2, r).start()
    S.smg[z, y, m] = s_in[...]
    S.qs[m] = q_in[m]
    S.us[m] = u_in[m]
    for layer in range(LAYERS):
        S.wd[layer, z, y] = d_in[layer]

    def join(staged, target):
        for xx in range(2):
            first_part = staged[2 * xx].astype(F32)
            second_part = staged[2 * xx + 1].astype(F32)
            for layer in range(LAYERS):
                cut = slice(layer * d_rows, (layer + 1) * d_rows)
                target[layer, z, xx, y] = jnp.concatenate(
                    [first_part[cut], second_part[cut]], axis=0
                ).astype(BF)

    side = lax.div(z, 2)
    inner = (z == 1) | (z == 2)
    outer = jnp.logical_not(inner)
    near_in, near_out = 1 + side, 3 * side
    far_in, far_out = 2 - side, 3 * (1 - side)
    buddy = near_in + near_out - z

    def at_z(z_at):
        return dev(z_at, x, y, c)

    LAST = -1
    DIRECT = 0

    def slab(cls, z_at, y_at):
        return (
            lambda: S.smg.at[z_at, y_at],
            lambda: S.wq.at[0, z_at, :, y_at],
            lambda: S.wog.at[z_at, y_at],
            lambda: S.wu.at[0, z_at, :, y_at],
            lambda: S.wd.at[0, z_at, y_at],
            lambda: S.wq.at[1, z_at, :, y_at],
            lambda: S.wu.at[1, z_at, :, y_at],
            lambda: S.wd.at[1, z_at, y_at],
        )[cls]()

    def z_copy(cls, n, z_at, to):
        spot = S.wd.at[1, z_at] if cls == LAST else slab(cls, z_at, y)
        return rcopy(spot, spot, S.gz_s.at[cls, n], S.gz_r.at[cls, z_at], at_z(to))

    def y_copy(cls, z_at):
        spot = slab(cls, z_at, y)
        return rcopy(spot, spot, S.gy_s.at[cls, z_at], S.gy_r.at[cls, z_at], across)

    def gather_direct(cls):
        z_copy(cls, 0, z, buddy).start()
        z_copy(cls, 1, z, far_in).start()
        if cls < DIRECT:
            z_copy(cls, 2, z, far_out).start()

    def gather_start(cls):
        if cls != LAST:
            gather_direct(cls)
        y_copy(cls, z).start()

    def gather_cross(cls):
        if cls != LAST:
            return
        spot = slab(cls, z, 1 - y)
        rcopy(spot, spot, S.gy_s.at[cls, z], S.gy_r.at[cls, z], across).wait_recv()
        gather_direct(cls)

    def gather_take(cls, z_at, relay):
        z_copy(cls, 0, z_at, buddy).wait_recv()
        if relay is not None:
            z_copy(cls, relay, z_at, near_out).start()
        if cls != LAST:
            y_copy(cls, z_at).start()

    def gather_relay(cls):
        gather_take(cls, buddy, None)
        if cls < DIRECT:
            gather_take(cls, far_in, None)
            gather_take(cls, far_out, None)
            return

        @pl.when(inner)
        def _():
            gather_take(cls, far_in, 2)

        gather_relay_far(cls)

    def gather_relay_far(cls):
        @pl.when(inner)
        def _():
            gather_take(cls, far_out, 3)

    def gather_end(cls):
        @pl.when(outer)
        def _():
            gather_take(cls, far_in, None)
            gather_take(cls, far_out, None)

    def gather_wait(cls):
        if cls == LAST:
            spot = S.wd.at[1, z]
            return

        def one(t):
            spot = slab(cls, t, 1 - y)
            rcopy(spot, spot, S.gy_s.at[cls, t], S.gy_r.at[cls, t], across).wait_recv()

        for t in (z, buddy, far_in, far_out):
            one(t)

    def gather_drain(cls):
        z_copy(cls, 0, z, buddy).wait_send()
        z_copy(cls, 1, z, far_in).wait_send()
        if cls < DIRECT:
            z_copy(cls, 2, z, far_out).wait_send()
        else:

            @pl.when(inner)
            def _():
                z_copy(cls, 2, far_in, near_out).wait_send()
                z_copy(cls, 3, far_out, near_out).wait_send()

        def one(t, carry):
            y_copy(cls, t).wait_send()
            return carry

        if cls == LAST:
            one(z, 0)
        else:
            lax.fori_loop(0, nz, one, 0)

    for r in range(3):
        stage_wait(1, r)
    join(S.qs, S.wq)
    gather_start(1)
    for r in range(3):
        stage_wait(0, r)
    gather_start(0)

    def x_spots(target, base, mine):
        return [target.at[pl.ds(base + block * (2 * k + mine), block)] for k in range(2)]

    def swap_start(which, target, base):
        for k, spot in enumerate(x_spots(target, base, x)):
            rcopy(spot, spot, S.inx_s.at[which, k], S.inx_r.at[which, k], peer).start()

    def swap_wait(which, target, base):
        for k, spot in enumerate(x_spots(target, base, 1 - x)):
            rcopy(spot, spot, S.inx_s.at[which, k], S.inx_r.at[which, k], peer).wait_recv()
        for k, spot in enumerate(x_spots(target, base, x)):
            rcopy(spot, spot, S.inx_s.at[which, k], S.inx_r.at[which, k], peer).wait_send()

    mine = half * c
    theirs = half * (1 - c)
    scatter_in_wait(0, inp, first, mine + block * x)
    swap_start(0, first, mine)
    for r in range(3):
        stage_wait(2, r)
    join(S.us, S.wu)
    gather_relay(1)
    gather_relay(0)
    swap_wait(0, first, mine)
    spot = first.at[pl.ds(mine, half)]
    rcopy(spot, spot, S.ins_s.at[0], S.ins_r.at[0], sibling).start()
    S.stream[...] = S.xf[0, pl.ds(mine, half), :].astype(F32)

    @pl.when(jnp.logical_not(perm_stays))
    def _():
        spot = S.wog.at[z, y]
        rcopy(spot, spot, S.perm.at[0], S.perm.at[1], peer).wait_recv()

    gather_start(2)
    gather_end(1)
    gather_end(0)
    gather_relay(2)
    gather_start(3)
    gather_wait(0)

    def small_params():
        row_shape = (devices * 16, D)
        lane = lax.broadcasted_iota(jnp.int32, (128, D), 0)
        col = lax.broadcasted_iota(jnp.int32, (128, D), 1)
        tile = jnp.where(lax.rem(col, d_rows) == lane, 1.0, 0.0).astype(BF)
        packs = S.smg[:, :, :, 0:16, :].reshape(devices * 16, 128)
        spread = dot_nn(packs, tile)
        owner_row = lax.broadcasted_iota(jnp.int32, row_shape, 0) >> 4
        zz = owner_row >> 3
        yy = (owner_row >> 2) & 1
        xx = (owner_row >> 1) & 1
        cc = owner_row & 1
        owner = zz * 8 + xx * 4 + yy * 2 + cc
        at = lax.div(lax.broadcasted_iota(jnp.int32, row_shape, 1), d_rows)
        spread = jnp.where(owner == at, spread, 0.0)
        S.pb[...] = jnp.sum(spread.reshape(devices, 16, D), axis=0)
        lane = lax.broadcasted_iota(jnp.int32, (128, ff), 0)
        col = lax.broadcasted_iota(jnp.int32, (128, ff), 1)
        tile = jnp.where(lax.rem(col, f_rows) == lane, 1.0, 0.0).astype(BF)
        packs = S.smg[:, :, m, 16:32, :].reshape(2 * nz * 16, 128)
        spread = dot_nn(packs, tile)
        row_shape = (2 * nz * 16, ff)
        owner = lax.broadcasted_iota(jnp.int32, row_shape, 0) >> 4
        at = lax.div(lax.broadcasted_iota(jnp.int32, row_shape, 1), f_rows)
        spread = jnp.where(owner == at, spread, 0.0)
        S.ub[...] = jnp.sum(spread.reshape(2 * nz, 16, ff), axis=0)
        source = lax.broadcasted_iota(jnp.int32, (D, PACK), 0)
        target, unused_q, unused_v = packed_lanes((D, PACK), 1)
        pick = jnp.where(source == target + m * (LOCAL_HEADS * HEAD_DIM), 1.0, 0.0).astype(BF)
        picked = dot_nn(S.pb[...].astype(BF), pick)
        unused, is_query, is_value = packed_lanes((1, PACK), 1)
        for layer in range(LAYERS):
            base = 8 * layer
            row = jnp.where(is_query, picked[base : base + 1], 0.0)
            row = jnp.where(is_value, picked[base + 3 : base + 4], row)
            S.bq[layer, 0:1, :] = row

    small_params()
    scatter_in(1, cot, S.ct, block * (2 * lax.rem(z, 2) + x))

    def param(layer, kind):
        return S.pb[8 * layer + kind : 8 * layer + kind + 1, :]

    def piece_rows(i):
        return pl.ds(i * PIECE if isinstance(i, int) else pl.multiple_of(i * PIECE, PIECE), PIECE)

    def own_rows(i):
        return pl.ds(pl.multiple_of(mine + i * PIECE, PIECE), PIECE)

    def other_rows(i):
        return pl.ds(pl.multiple_of(theirs + i * PIECE, PIECE), PIECE)

    every = slice(None)

    def load_both(ref, i, cols=every):
        return jnp.concatenate([ref[other_rows(i), cols], ref[own_rows(i), cols]], axis=0)

    def store_both(ref, i, value, cols=every):
        ref[other_rows(i), cols] = value[:PIECE]
        ref[own_rows(i), cols] = value[PIECE:]

    def spread_start(par, i, ref, value):
        ref[own_rows(i), :] = value
        spot = ref.at[own_rows(i)]
        rcopy(spot, spot, S.ag_s.at[par, i], S.ag_r.at[par, i], sibling).start()

    def spread_wait(par, i, ref):
        got = ref.at[other_rows(i)]
        sent = ref.at[own_rows(i)]
        rcopy(got, got, S.ag_s.at[par, i], S.ag_r.at[par, i], sibling).wait_recv()
        rcopy(sent, sent, S.ag_s.at[par, i], S.ag_r.at[par, i], sibling).wait_send()

    def sib_copy(par, i):
        at = piece_rows(i)
        return rcopy(
            S.sibs.at[par, at], S.sibr.at[par, at], S.sib_s.at[par, i], S.sib_r.at[par, i], sibling
        )

    def peer_copy(par, i):
        at = piece_rows(i)
        return rcopy(S.xs.at[par, at], S.xr.at[par, at], S.x_s.at[par, i], S.x_r.at[par, i], peer)

    def part_send(par, i, value):
        at = piece_rows(i)
        S.sibs[par, at, :] = value[:PIECE].astype(BF)
        sib_copy(par, i).start()
        S.ownp[at, :] = value[PIECE:]

    def part_pass(par, i):
        at = piece_rows(i)
        sib_copy(par, i).wait_recv()
        S.xs[par, at, :] = (S.ownp[at, :] + S.sibr[par, at, :].astype(F32)).astype(BF)
        peer_copy(par, i).start()

    def part_take(par, i):
        at = piece_rows(i)
        peer_copy(par, i).wait_recv()
        return S.xs[par, at, :].astype(F32) + S.xr[par, at, :].astype(F32)

    def part_drain(par):
        for i in range(pieces):
            sib_copy(par, i).wait_send()
            peer_copy(par, i).wait_send()

    def pipeline(stages, between=None):
        def one(step, carry):
            for lag, stage in enumerate(stages):
                if len(stages) == 1:
                    stage(step)
                    continue

                @pl.when((step >= lag) & (step < pieces + lag))
                def _():
                    stage(step - lag)

            for after, calls in (between or {}).items():

                @pl.when(step == after)
                def _():
                    for call in calls:
                        call()

            return carry

        lax.fori_loop(0, pieces + len(stages) - 1, one, 0)

    def norm_piece(total, at, layer, gain, shift, scaled_ref, inv_ref):
        centred = total - jnp.mean(total, axis=1, keepdims=True)
        inv = lax.rsqrt(jnp.mean(centred * centred, axis=1, keepdims=True) + 1e-12)
        scaled = centred * inv
        scaled_ref[layer, at, :] = scaled
        inv_ref[layer, at, :] = jnp.broadcast_to(inv, (PIECE, 128))
        return scaled * gain + shift

    def flat(value):
        return value.reshape(-1, value.shape[-1])

    def swap_lanes(value):
        return pltpu.roll(value.astype(F32), HEAD_DIM, 1).astype(BF)

    def mask_queries(queries, h):
        keep = jnp.logical_not(lane_low) if h == 1 else lane_low
        return jnp.where(keep, queries * jnp.asarray(HEAD_DIM**-0.5, BF), jnp.zeros((), BF))

    def query_cols(h):
        return slice(0, 128) if h < 2 else slice(384, 512)

    def head_keys(layer, h):
        if h < 2:
            return S.qkv[layer, :, 128:256]
        return swap_lanes(S.qkv[layer, :, 384:512])

    def head_values(layer, h):
        return S.qkv[layer, :, 256:384] if h < 2 else S.qkv[layer, :, 512:640]

    def project(layer, i):
        value = dot_nn(load_both(S.xf.at[layer], i), flat(S.wq[layer])) + S.bq[layer, 0:1, :]
        store_both(S.qkv.at[layer], i, value.astype(BF))

    def attend(layer, i):
        mixes = []
        for h in range(LOCAL_HEADS):
            queries = mask_queries(load_both(S.qkv.at[layer], i, query_cols(h)), h)
            scores = dot_nt(queries, head_keys(layer, h))
            weights = jnp.exp(scores - jnp.max(scores, axis=1, keepdims=True))
            weights = (weights * (1.0 / jnp.sum(weights, axis=1, keepdims=True))).astype(BF)
            store_both(S.prob.at[layer, h], i, weights)
            mixes.append(dot_nn(weights, head_values(layer, h)))
        mix = jnp.concatenate(
            [jnp.where(lane_low, mixes[0], mixes[1]), jnp.where(lane_low, mixes[2], 0.0)], axis=1
        )
        store_both(S.mix.at[layer], i, mix)
        store_both(S.mixl.at[layer], i, mix.astype(BF))
        part_send(0, i, dot_nn(mix.astype(BF), S.wo[layer]))

    def after_attention(layer, i):
        at = piece_rows(i)
        total = S.stream[at, :] + part_take(0, i) + param(layer, 1)
        normed = norm_piece(total, at, layer, param(layer, 4), param(layer, 6), S.xh1, S.iv1)
        S.normed[at, :] = normed
        spread_start(0, i, S.nl.at[layer], normed.astype(BF))

    def raise_part(layer, i):
        spread_wait(0, i, S.nl.at[layer])
        rounded = load_both(S.nl.at[layer], i)
        upward = dot_nn(rounded, flat(S.wu[layer])) + S.ub[layer : layer + 1, :]
        cdf = 0.5 * (1.0 + lax.erf(upward * (0.5**0.5)))
        density = jnp.exp(-0.5 * upward * upward) * ((2.0 * jnp.pi) ** -0.5)
        store_both(S.act.at[layer], i, (upward * cdf).astype(BF))
        store_both(S.gp.at[layer], i, cdf + upward * density)

    def lower_part(layer, i):
        part_send(1, i, dot_nn(load_both(S.act.at[layer], i), flat(S.wd[layer])))

    def after_lower(layer, i):
        at = piece_rows(i)
        total = S.normed[at, :] + part_take(1, i) + param(layer, 2)
        result = norm_piece(total, at, layer, param(layer, 5), param(layer, 7), S.xh2, S.iv2)
        if layer < LAYERS - 1:
            S.stream[at, :] = result
            spread_start(1, i, S.xf.at[layer + 1], result.astype(BF))
        else:
            S.back[0, at, :] = result.astype(BF)

    def next_project(layer, i):
        spread_wait(1, i, S.xf.at[layer])
        project(layer, i)

    def scatter_out(which, source):
        for k in range(2):
            stays = (2 * c + k == z) & (lax.div(z, 2) == c)
            spot = source.at[pl.ds(pl.multiple_of(block * (2 * k + x), block), block)]
            slot = lax.rem(z, 2)

            @pl.when(stays)
            def _():
                S.land[which, slot] = spot[...]

            @pl.when(jnp.logical_not(stays))
            def _():
                rcopy(
                    spot,
                    S.land.at[which, slot],
                    S.in_s.at[2 + which, k],
                    S.in_r.at[2 + which, slot],
                    dev(2 * c + k, x, y, lax.div(z, 2)),
                ).start()

    def scatter_out_wait(which, source, result):
        for k in range(2):
            spot = source.at[pl.ds(pl.multiple_of(block * (2 * k + x), block), block)]

            @pl.when(jnp.logical_not((2 * c + k == z) & (lax.div(z, 2) == c)))
            def _():
                rcopy(
                    spot, spot, S.in_s.at[2 + which, k], S.in_r.at[2 + which, 0], peer
                ).wait_send()

            @pl.when(jnp.logical_not(own_block(k)))
            def _():
                landed = S.land.at[which, k]
                rcopy(
                    landed, landed, S.in_s.at[2 + which, 0], S.in_r.at[2 + which, k], peer
                ).wait_recv()

        result[...] = S.land[which]

    def out_weights():
        gather_wait(2)
        for layer in range(LAYERS):
            cut = slice(layer * d_rows, (layer + 1) * d_rows)
            parts = [S.wog[t, yy].astype(F32)[cut] for t in range(nz) for yy in range(2)]
            parts.append(jnp.zeros((256 - 2 * nz * d_rows, D), F32))
            S.wo[layer] = jnp.concatenate(parts, axis=0).astype(BF)

    spot = first.at[pl.ds(theirs, half)]
    rcopy(spot, spot, S.ins_s.at[0], S.ins_r.at[0], sibling).wait_recv()
    gather_wait(1)
    for i in range(pieces):
        project(0, i)
    gather_start(4)
    gather_end(2)
    gather_relay(3)
    out_weights()
    pipeline(
        (lambda i: attend(0, i), lambda i: part_pass(0, i)),
        {1: [lambda: gather_end(3)], 2: [lambda: gather_start(5)], 3: [lambda: gather_relay(4)]},
    )
    pipeline((lambda i: after_attention(0, i),))
    part_drain(0)
    gather_start(6)
    gather_end(4)
    gather_wait(3)
    pipeline((lambda i: raise_part(0, i),))
    scatter_in_wait(1, cot, S.ct, block * x)
    gather_relay(5)
    gather_start(7)
    gather_end(5)
    gather_wait(4)
    pipeline((lambda i: lower_part(0, i), lambda i: part_pass(1, i)))
    swap_start(1, S.ct, 0)
    gather_relay(6)
    gather_wait(5)
    pipeline(
        (lambda i: after_lower(0, i), lambda i: next_project(1, i)),
        {0: [lambda: gather_end(6)], 3: [lambda: gather_cross(7)]},
    )
    part_drain(1)
    pipeline(
        (lambda i: attend(1, i), lambda i: part_pass(0, i)),
        {1: [lambda: gather_relay(7)], 3: [lambda: gather_end(7)]},
    )
    gather_wait(6)
    pipeline(
        (
            lambda i: after_attention(1, i),
            lambda i: raise_part(1, i),
            lambda i: lower_part(1, i),
            lambda i: part_pass(1, i),
        ),
        {1: [lambda: gather_wait(7)]},
    )
    part_drain(0)
    swap_wait(1, S.ct, 0)


    def add_row(layer, kind, value):
        S.sg[layer, kind : kind + 1, :] += jnp.sum(value, axis=0, keepdims=True)

    def norm_back_piece(grad, at, layer, which):
        scaled = (S.xh1 if which == 0 else S.xh2)[layer, at, :]
        inv = (S.iv1 if which == 0 else S.iv2)[layer, at, 0:1]
        add_row(layer, 2 + which, grad * scaled)
        add_row(layer, 4 + which, grad)
        weighted = grad * param(layer, 4 + which)
        back = (
            weighted
            - jnp.mean(weighted, axis=1, keepdims=True)
            - scaled * jnp.mean(weighted * scaled, axis=1, keepdims=True)
        ) * inv
        return back

    def lower_back(layer, i, grad):
        at = piece_rows(i)
        back = norm_back_piece(grad, at, layer, 1)
        S.normed[at, :] = back
        rounded = back.astype(BF)
        add_row(layer, 1, rounded.astype(F32))
        spread_start(0, i, S.dl, rounded)

    def raise_back(layer, i):
        spread_wait(0, i, S.dl)
        back = dot_nt(load_both(S.dl, i), flat(S.wd[layer])) * load_both(S.gp.at[layer], i)
        rounded = back.astype(BF)
        store_both(S.du, i, rounded)
        add_row(layer, 6, rounded.astype(F32))
        part_send(0, i, dot_nt(rounded, flat(S.wu[layer])))

    grads = (S.gq, S.gu, S.gd, S.go)
    from_y = (S.ryq, S.ryu, None, S.ryo)
    from_z = (S.rzq, S.rzu, None, S.rzo)

    def grad_slab(layer, kind, t, y_at):
        ref = grads[kind]
        return ref.at[layer, t, :, y_at] if kind < 2 else ref.at[layer, t, y_at]

    def z_first(layer, kind):
        return kind == 2 and layer == LAYERS - 1

    def z_slab(layer, kind, t):
        return S.gd.at[layer, t] if z_first(layer, kind) else grad_slab(layer, kind, t, y)

    def y_landing(layer, kind):
        if kind == 2:
            return S.ryl if z_first(layer, kind) else S.ryd
        return from_y[kind].at[layer]

    def z_landing(layer, kind, slot):
        if kind == 2:
            return (S.rzl if z_first(layer, kind) else S.rzd).at[slot]
        return from_z[kind].at[layer, slot]

    def reduce_y_copy(layer, kind):
        ref = grads[kind]
        if z_first(layer, kind):
            source = S.syl
        else:
            source = ref.at[layer, :, :, 1 - y] if kind < 2 else ref.at[layer, :, 1 - y]
        n = 4 * layer + kind
        return rcopy(source, y_landing(layer, kind), S.ry_s.at[n], S.ry_r.at[n], across)

    def reduce_z_copy(layer, kind, t, slot, to):
        n = 4 * layer + kind
        return rcopy(
            z_slab(layer, kind, t),
            z_landing(layer, kind, slot),
            S.rz_s.at[n, t],
            S.rz_r.at[n, slot],
            at_z(to),
        )

    def slab_add(target, other):
        if len(target.shape) == 3:
            for xx in range(2):
                target[xx] = (target[xx].astype(F32) + other[xx].astype(F32)).astype(BF)
        else:
            target[...] = (target[...].astype(F32) + other[...].astype(F32)).astype(BF)

    def reduce_direct(layer, kind):
        @pl.when(outer)
        def _():
            reduce_z_copy(layer, kind, far_in, 2, buddy).start()
            reduce_z_copy(layer, kind, far_out, 3, buddy).start()

        reduce_z_copy(layer, kind, buddy, 0, buddy).start()

    def reduce_start(layer, kind):
        if z_first(layer, kind):
            reduce_direct(layer, kind)
        else:
            reduce_y_copy(layer, kind).start()

    def reduce_first(layer, kind):
        reduce_y_copy(layer, kind).wait_recv()

        def one(t, carry):
            slab_add(grad_slab(layer, kind, t, y), y_landing(layer, kind).at[t])
            return carry

        lax.fori_loop(0, nz, one, 0)
        reduce_direct(layer, kind)

    def reduce_relay(layer, kind):
        @pl.when(inner)
        def _():
            for slot, t in ((2, far_in), (3, far_out)):
                reduce_z_copy(layer, kind, t, slot, buddy).wait_recv()
                slab_add(z_slab(layer, kind, t), z_landing(layer, kind, slot))
                reduce_z_copy(layer, kind, t, 1, t).start()

    def reduce_cross(layer):
        d_out[layer] = S.gd[layer, z, y].astype(F32)
        other = S.gd[layer, z, 1 - y].astype(F32)
        for slot in (0, 1):
            reduce_z_copy(layer, 2, z, slot, buddy).wait_recv()
            d_out[layer] += S.rzl[slot, y].astype(F32)
            other = other + S.rzl[slot, 1 - y].astype(F32)
        S.syl[...] = other.astype(BF)
        reduce_y_copy(layer, 2).start()

    def reduce_last_d(layer):
        reduce_y_copy(layer, 2).wait_recv()
        d_out[layer] += S.ryl[...].astype(F32)

    final = (S.fq, S.fu, d_out, S.fo)

    def reduce_last(layer, kind):
        if kind == 3:
            target = S.fo.at[layer]
            cut = lambda value: value[0:d_rows]
        else:
            target = final[kind].at[layer]
            cut = lambda value: value
        target[...] = cut(grad_slab(layer, kind, z, y)[...].astype(F32))

        for slot in (0, 1):
            reduce_z_copy(layer, kind, z, slot, buddy).wait_recv()
            target[...] += cut(z_landing(layer, kind, slot)[...].astype(F32))

        if kind < 2:
            result = (S.oq, S.ou)[kind]
            for r in (1, 2, 0):
                hand_copy(layer, kind, r).start()
            for xx in range(2):
                for cc in range(2):

                    @pl.when((x == xx) & (c == cc))
                    def _():
                        result[layer, 2 * xx + cc] = target[xx, cc * d_rows : (cc + 1) * d_rows, :]

        if kind == 3:
            @pl.when(owner_stays)
            def _():
                S.oo[layer] = target[...]

            @pl.when(jnp.logical_not(owner_stays))
            def _():
                owner_copy(layer).start()

    def hand_copy(layer, kind, r):
        x_r, c_r = relation[r]
        source = (S.fq, S.fu)[kind].at[
            layer, x_r, pl.ds(pl.multiple_of(c_r * d_rows, 8), d_rows)
        ]
        target = (S.oq, S.ou)[kind].at[layer, m]
        return rcopy(
            source,
            target,
            S.fin_s.at[layer, kind, r],
            S.fin_r.at[layer, kind, r],
            dev(z, x_r, y, c_r),
        )

    owner_to = dev(2 * x + c, lax.div(z, 2), lax.rem(z, 2), y)
    owner_stays = (2 * x + c == z) & (lax.div(z, 2) == x) & (lax.rem(z, 2) == y) & (y == c)

    def owner_copy(layer):
        return rcopy(
            S.fo.at[layer], S.oo.at[layer], S.fino.at[layer, 0], S.fino.at[layer, 1], owner_to
        )

    def reduce_drain(layer, kind):
        reduce_y_copy(layer, kind).wait_send()
        for t in range(nz):

            @pl.when(z != t)
            def _():
                reduce_z_copy(layer, kind, t, 0, buddy).wait_send()

        if kind < 2:
            for r in range(3):
                hand_copy(layer, kind, r).wait_send()
        if kind == 3:
            @pl.when(jnp.logical_not(owner_stays))
            def _():
                owner_copy(layer).wait_send()
                owner_copy(layer).wait_recv()

    def lower_grad(layer):
        for i in range(2):
            value = dot_tn(S.act[layer, :, i * (ff // 2) : (i + 1) * (ff // 2)], S.dl[...])
            S.gd[layer, i * (nz // 2) : (i + 1) * (nz // 2)] = value.astype(BF).reshape(
                nz // 2, 2, f_rows, D
            )
        reduce_start(layer, 2)

    def raise_grad(layer):
        for i in range(2):
            value = dot_tn(S.nl[layer, :, i * (D // 2) : (i + 1) * (D // 2)], S.du[...])
            S.gu[layer, i * (nz // 2) : (i + 1) * (nz // 2)] = value.astype(BF).reshape(
                nz // 2, 2, 2, two, ff
            )
        reduce_start(layer, 1)

    def out_grad(layer):
        value = dot_tn(S.mixl[layer], S.db[...])
        empty = jnp.zeros((32 - d_rows, D), F32)
        for t in range(nz):
            for yy in range(2):
                at = (2 * t + yy) * d_rows
                S.go[layer, t, yy] = jnp.concatenate(
                    [value[at : at + d_rows], empty], axis=0
                ).astype(BF)
        reduce_start(layer, 3)

    def project_grad(layer):
        for i in range(2):
            value = dot_tn(S.xf[layer, :, i * (D // 2) : (i + 1) * (D // 2)], S.dq[...])
            S.gq[layer, i * (nz // 2) : (i + 1) * (nz // 2)] = value.astype(BF).reshape(
                nz // 2, 2, 2, two, PACK
            )
        reduce_start(layer, 0)

    def branch_back(layer, i):
        at = piece_rows(i)
        back = norm_back_piece(part_take(0, i) + S.normed[at, :], at, layer, 0)
        S.stream[at, :] = back
        rounded = back.astype(BF)
        add_row(layer, 0, rounded.astype(F32))
        spread_start(1, i, S.db, rounded)

    scale = HEAD_DIM**-0.5

    def attend_back(layer, i):
        spread_wait(1, i, S.db)
        grad_mix = dot_nt(load_both(S.db, i), S.wo[layer]).astype(BF)
        store_both(S.dm, i, grad_mix)
        mix = load_both(S.mix.at[layer], i)
        results = []
        for h in range(LOCAL_HEADS):
            keep = jnp.logical_not(lane_low) if h == 1 else lane_low
            cols = slice(0, 128) if h < 2 else slice(128, 256)
            grad = jnp.where(keep, grad_mix[:, cols], jnp.zeros((), BF))
            delta = jnp.sum(grad.astype(F32) * mix[:, cols], axis=1, keepdims=True)
            grad_weights = dot_nt(grad, head_values(layer, h))
            weights = load_both(S.prob.at[layer, h], i).astype(F32)
            rounded = (weights * (grad_weights - delta)).astype(BF)
            store_both(S.ds.at[h], i, rounded)
            results.append((dot_nn(rounded, head_keys(layer, h)) * scale).astype(BF))
        store_both(S.dq, i, jnp.where(lane_low, results[0], results[1]), slice(0, 128))
        store_both(S.dq, i, results[2], slice(384, 512))

    def attend_back_end(layer):
        keys_back, values_back = [], []
        for h in range(LOCAL_HEADS):
            cols = slice(0, 128) if h < 2 else slice(128, 256)
            queries = mask_queries(S.qkv[layer, :, query_cols(h)], h)
            keys_back.append(dot_tn(S.ds[h], queries).astype(BF))
            values_back.append(dot_tn(S.prob[layer, h], S.dm[:, cols]).astype(BF))
        S.dq[:, 128:256] = jnp.where(lane_low, keys_back[0], keys_back[1])
        S.dq[:, 256:384] = jnp.where(lane_low, values_back[0], values_back[1])
        S.dq[:, 384:512] = jnp.where(lane_low, S.dq[:, 384:512], swap_lanes(keys_back[2]))
        S.dq[:, 512:640] = jnp.where(lane_low, values_back[2], jnp.zeros((), BF))
        S.sg[layer, 7:8, 0:PACK] = jnp.sum(S.dq[...].astype(F32), axis=0, keepdims=True)

    def project_back(layer, i):
        part_send(1, i, dot_nt(load_both(S.dq, i), flat(S.wq[layer])))

    def next_back(layer, i):
        at = piece_rows(i)
        grad = part_take(1, i) + S.stream[at, :]
        if layer > 0:
            lower_back(layer - 1, i, grad)
        else:
            S.back[1, at, :] = grad.astype(BF)

    def small_y(layer):
        return rcopy(S.sg.at[layer], S.sgy.at[layer], S.sgy_s.at[layer], S.sgy_r.at[layer], across)

    def small_z(layer, k):
        to = dev(lax.rem(z + k, nz), x, y, c)
        return rcopy(
            S.sgt.at[layer], S.sgz.at[layer, k], S.sgz_s.at[layer, k], S.sgz_r.at[layer, k], to
        )

    def small_member(layer, r):
        x_r, c_r = relation[r]
        return rcopy(
            S.sgt.at[layer],
            S.sga.at[layer, m],
            S.sga_s.at[layer, r],
            S.sga_r.at[layer, r],
            dev(z, x_r, y, c_r),
        )

    def small_one(layer):
        small_y(layer).start()

    def small_two(layer):
        small_y(layer).wait_recv()
        S.sgt[layer] = S.sg[layer] + S.sgy[layer]
        for k in range(1, nz):
            small_z(layer, k).start()

    def small_three(layer):
        for k in range(1, nz):
            small_z(layer, k).wait_recv()
        for k in range(1, nz):
            small_z(layer, k).wait_send()
        total = S.sgt[layer]
        for k in range(1, nz):
            total = total + S.sgz[layer, k]
        S.sgt[layer] = total
        for r in range(3):
            small_member(layer, r).start()
        S.sga[layer, m] = total

    def small_four(layer):
        for r in range(3):
            small_member(layer, r).wait_send()
            small_member(layer, r).wait_recv()
        small_y(layer).wait_send()
        lane = lax.broadcasted_iota(jnp.int32, (D, 128), 1)
        col = lax.broadcasted_iota(jnp.int32, (D, 128), 0)
        narrow = lane < d_rows
        pick = jnp.where((col == d_rows * d + lane) & narrow, 1.0, 0.0)
        both = S.sga[layer, 2 * x] + S.sga[layer, 2 * x + 1]
        found = dot_exact(both, pick)[:, 0:d_rows]
        g_biases[layer, 1:3, :] = found[0:2]
        g_gains[layer] = found[2:4]
        g_shifts[layer] = found[4:6]
        dim, is_query, is_value = packed_lanes((D, 128), 0)
        hit = (dim == d_rows * (d - 8 * z) + lane) & narrow
        attn = S.sga[layer, z]
        found = dot_exact(attn, jnp.where(hit & is_query, 1.0, 0.0))
        g_biases[layer, 0:1, :] = found[7:8, 0:d_rows]
        found = dot_exact(attn, jnp.where(hit & is_value, 1.0, 0.0))
        g_value[layer : layer + 1, :] = found[7:8, 0:d_rows]
        pick = jnp.where((col == f_rows * (2 * z + y) + lane) & (lane < f_rows), 1.0, 0.0)
        found = dot_exact(S.sga[layer, m], pick)
        g_raise[layer : layer + 1, :] = found[6:7, 0:f_rows]

    def hand_wait(layer, kind):
        for r in range(3):
            hand_copy(layer, kind, r).wait_recv()

    def unpack_heads(layer):
        hand_wait(layer, 0)
        for pair in range(2):
            even = [S.oq[layer, 2 * pair, :, 128 * t : 128 * t + 128] for t in range(5)]
            odd = [S.oq[layer, 2 * pair + 1, :, 128 * t : 128 * t + 128] for t in range(5)]
            thirds = (
                (even[3], turn(odd[3])),
                (turn(even[3]), odd[3]),
                (even[4], turn(odd[4])),
            )
            for kind in range(3):
                turned = turn(odd[kind])
                tiles = [
                    even[kind],
                    jnp.where(lane_low, thirds[kind][0], turned),
                    jnp.where(lane_low, turned, thirds[kind][1]),
                ]
                base = 384 * pair
                g_qkv[layer, kind, :, base : base + 384] = jnp.concatenate(tiles, axis=1)

    def unpack_raise(layer):
        hand_wait(layer, 1)
        wide = [S.ou[layer, member] for member in range(MEMBERS)]
        parts = []
        for z_at in range(nz):
            for x_at in range(2):
                for y_at in range(2):
                    for c_at in range(2):
                        at = (2 * z_at + y_at) * f_rows
                        parts.append(wide[2 * x_at + c_at][:, at : at + f_rows])
        g_up[layer] = jnp.concatenate(parts, axis=1)

    S.sg[...] = jnp.zeros_like(S.sg)

    def turn_back(i):
        after_lower(1, i)
        lower_back(1, i, S.ct[piece_rows(i), :].astype(F32))

    pipeline(
        (turn_back, lambda i: raise_back(1, i), lambda i: part_pass(0, i)),
        {4: [lambda: lower_grad(1)]},
    )
    part_drain(1)
    raise_grad(1)
    scatter_out(0, S.back.at[0])
    pipeline((lambda i: branch_back(1, i), lambda i: attend_back(1, i)))
    part_drain(0)
    attend_back_end(1)
    pipeline((lambda i: project_back(1, i), lambda i: part_pass(1, i)))
    small_one(1)
    project_grad(1)
    out_grad(1)
    reduce_first(1, 1)
    pipeline(
        (
            lambda i: next_back(1, i),
            lambda i: raise_back(0, i),
            lambda i: part_pass(0, i),
        ),
        {1: [lambda: reduce_relay(1, 2)], 4: [lambda: lower_grad(0)]},
    )
    part_drain(1)
    reduce_first(1, 0)
    raise_grad(0)
    pipeline(
        (lambda i: branch_back(0, i), lambda i: attend_back(0, i)),
        {1: [lambda: reduce_relay(1, 1)], 3: [lambda: reduce_first(1, 3)]},
    )
    part_drain(0)
    attend_back_end(0)
    reduce_cross(1)
    small_one(0)
    pipeline((lambda i: project_back(0, i), lambda i: part_pass(1, i)))
    project_grad(0)
    out_grad(0)
    reduce_relay(1, 0)
    small_two(1)
    pipeline((lambda i: next_back(0, i),), {1: [lambda: reduce_relay(1, 3)]})
    part_drain(1)
    scatter_out(1, S.back.at[1])
    reduce_first(0, 2)
    small_three(1)
    reduce_last(1, 1)
    reduce_last(1, 0)
    reduce_first(0, 1)
    reduce_relay(0, 2)
    reduce_last(1, 3)
    small_two(0)
    reduce_last_d(1)
    small_four(1)
    reduce_first(0, 0)
    reduce_relay(0, 1)
    small_three(0)
    reduce_first(0, 3)
    reduce_last(0, 2)
    reduce_relay(0, 0)
    reduce_last(0, 1)
    reduce_relay(0, 3)
    small_four(0)
    unpack_heads(1)
    unpack_raise(1)
    reduce_last(0, 0)
    reduce_last(0, 3)

    for kind in range(3):
        for r in range(3):
            stage_copy(kind, r).wait_send()
    scatter_in_drain(0, inp, first)
    scatter_in_drain(1, cot, S.ct)

    @pl.when(jnp.logical_not(perm_stays))
    def _():
        perm_copy.wait_send()

    spot = first.at[pl.ds(mine, half)]
    rcopy(spot, spot, S.ins_s.at[0], S.ins_r.at[0], sibling).wait_send()
    for cls in range(8):
        gather_drain(cls)
    scatter_out_wait(0, S.back.at[0], out)
    scatter_out_wait(1, S.back.at[1], gin)
    for layer in range(LAYERS):
        for kind in range(4):
            reduce_drain(layer, kind)
    unpack_raise(0)
    unpack_heads(0)
    o_out[...] = S.oo[...]


def hand_over(*refs):
    for n in range(11):
        refs[n + 11][...] = refs[n][...]


def grouped(nz, ny):
    def run(inputs, w_qkv, w_out, w_up, w_down, biases, value_bias, up_bias, gains, shifts, cotangent):
        block = inputs.shape[1]
        d_rows = w_out.shape[1]
        f_rows = w_down.shape[1]
        rows = 2 * nz * block
        half = rows // 2
        layout = scratch_layout(nz, ny, rows, half, d_rows, f_rows)
        vmem = pl.BlockSpec(memory_space=pltpu.VMEM)
        weights = (w_qkv, w_out, w_up, w_down, biases, value_bias, up_bias, gains, shifts)
        shapes = [jax.ShapeDtypeStruct(inputs.shape, BF)] * 2
        shapes += [jax.ShapeDtypeStruct(array.shape, F32) for array in weights]
        results = pl.pallas_call(
            functools.partial(group_kernel, layout, nz),
            out_shape=tuple(shapes),
            in_specs=[vmem] * 11,
            out_specs=[vmem] * 11,
            scratch_shapes=list(layout.values()),
            compiler_params=pltpu.CompilerParams(
                collective_id=0, has_side_effects=True, vmem_limit_bytes=KERNEL_VMEM
            ),
        )(inputs, *weights, cotangent)
        return pl.pallas_call(
            hand_over,
            out_shape=tuple(shapes),
            in_specs=[vmem] * 11,
            out_specs=[vmem] * 11,
        )(*results)

    return run


def part_count(row_count):
    count = 1
    while row_count % count != 0 or row_count // count > 2048:
        count = count + 1
    return count


def exact_gelu(values):
    return jax.nn.gelu(values, approximate=False)


def normalize(values, gain, shift):
    centred = values - jnp.mean(values, axis=1, keepdims=True)
    inv_std = lax.rsqrt(jnp.mean(centred * centred, axis=1, keepdims=True) + 1e-12)
    scaled = centred * inv_std
    return (scaled * gain + shift, scaled, inv_std)


def norm_back(grad, scaled, inv_std, gain):
    weighted = grad * gain
    return (
        weighted
        - jnp.mean(weighted, axis=1, keepdims=True)
        - scaled * jnp.mean(weighted * scaled, axis=1, keepdims=True)
    ) * inv_std


def split_heads(seq_array, count):
    seq_count, width, unused = seq_array.shape
    return seq_array.reshape(seq_count, count, width // count, HEADS, HEAD_DIM).transpose(
        1, 0, 2, 3, 4
    )


def merge_heads(head_array):
    seq_count, unused, row_count, unused_dim = head_array.shape
    return head_array.transpose(0, 2, 1, 3).reshape(seq_count * row_count, HEADS * HEAD_DIM)


def attend_forward(queries, keys, values):
    seq_count, row_count, unused = queries.shape
    factor = HEAD_DIM ** (-0.5)
    query_heads = queries.reshape(seq_count, row_count, HEADS, HEAD_DIM)
    start_state = (
        jnp.full((seq_count, HEADS, row_count), -1e30, jnp.float32),
        jnp.zeros((seq_count, HEADS, row_count), jnp.float32),
        jnp.zeros((seq_count, HEADS, row_count, HEAD_DIM), jnp.float32),
    )
    piece = (
        lax.all_gather(keys, "ctx", axis=1, tiled=True),
        lax.all_gather(values, "ctx", axis=1, tiled=True),
    )
    count = part_count(piece[0].shape[1])

    def attend_advance(inner, parts):
        peak, totals, accum = inner
        key_part, value_part = parts
        scores = (
            jnp.einsum("sthd,skhd->shtk", query_heads, key_part, preferred_element_type=jnp.float32)
            * factor
        )
        new_peak = jnp.maximum(peak, jnp.max(scores, axis=3))
        decay = jnp.exp(peak - new_peak)
        weights = jnp.exp(scores - new_peak[..., None])
        totals = totals * decay + jnp.sum(weights, axis=3)
        accum = accum * decay[..., None] + jnp.einsum(
            "shtk,skhd->shtd",
            weights.astype(jnp.bfloat16),
            value_part,
            preferred_element_type=jnp.float32,
        )
        return ((new_peak, totals, accum), None)

    result, _ = lax.scan(
        attend_advance, start_state, (split_heads(piece[0], count), split_heads(piece[1], count))
    )
    peak, totals, accum = result
    mixed = merge_heads(accum / totals[..., None])
    return (mixed, peak + jnp.log(totals))


def query_fold(queries, grad_mixed, logsum, row_delta, keys, values):
    seq_count, row_count, unused = queries.shape
    factor = HEAD_DIM ** (-0.5)
    query_heads = queries.reshape(seq_count, row_count, HEADS, HEAD_DIM)
    grad_heads = grad_mixed.reshape(seq_count, row_count, HEADS, HEAD_DIM)
    start_state = jnp.zeros((seq_count, HEADS, row_count, HEAD_DIM), jnp.float32)
    piece = (
        lax.all_gather(keys, "ctx", axis=1, tiled=True),
        lax.all_gather(values, "ctx", axis=1, tiled=True),
    )
    count = part_count(piece[0].shape[1])

    def query_advance(totals, parts):
        key_part, value_part = parts
        scores = (
            jnp.einsum("sthd,skhd->shtk", query_heads, key_part, preferred_element_type=jnp.float32)
            * factor
        )
        weights = jnp.exp(scores - logsum[..., None])
        grad_weights = jnp.einsum(
            "sthd,skhd->shtk", grad_heads, value_part, preferred_element_type=jnp.float32
        )
        grad_scores = (weights * (grad_weights - row_delta[..., None])).astype(jnp.bfloat16)
        return (
            totals
            + jnp.einsum(
                "shtk,skhd->shtd", grad_scores, key_part, preferred_element_type=jnp.float32
            )
            * factor,
            None,
        )

    result, _ = lax.scan(
        query_advance, start_state, (split_heads(piece[0], count), split_heads(piece[1], count))
    )
    return result


def key_fold(queries, grad_mixed, keys, values, all_logsum, all_delta):
    seq_count, row_count, unused = keys.shape
    factor = HEAD_DIM ** (-0.5)
    key_heads = keys.reshape(seq_count, row_count, HEADS, HEAD_DIM)
    value_heads = values.reshape(seq_count, row_count, HEADS, HEAD_DIM)
    start_state = (
        jnp.zeros((seq_count, HEADS, row_count, HEAD_DIM), jnp.float32),
        jnp.zeros((seq_count, HEADS, row_count, HEAD_DIM), jnp.float32),
    )
    piece = (
        lax.all_gather(queries, "ctx", axis=1, tiled=True),
        lax.all_gather(grad_mixed, "ctx", axis=1, tiled=True),
    )
    width = piece[0].shape[1]
    count = part_count(width)
    block = width // count
    log_parts = all_logsum.reshape(seq_count, HEADS, count, block).transpose(2, 0, 1, 3)
    delta_parts = all_delta.reshape(seq_count, HEADS, count, block).transpose(2, 0, 1, 3)

    def key_advance(inner, parts):
        grad_keys, grad_values = inner
        query_part, grad_part, log_part, delta_part = parts
        scores = (
            jnp.einsum("sqhd,skhd->shqk", query_part, key_heads, preferred_element_type=jnp.float32)
            * factor
        )
        weights = jnp.exp(scores - log_part[..., None])
        grad_values = grad_values + jnp.einsum(
            "shqk,sqhd->shkd",
            weights.astype(jnp.bfloat16),
            grad_part,
            preferred_element_type=jnp.float32,
        )
        grad_weights = jnp.einsum(
            "sqhd,skhd->shqk", grad_part, value_heads, preferred_element_type=jnp.float32
        )
        grad_scores = (weights * (grad_weights - delta_part[..., None])).astype(jnp.bfloat16)
        grad_keys = (
            grad_keys
            + jnp.einsum(
                "shqk,sqhd->shkd", grad_scores, query_part, preferred_element_type=jnp.float32
            )
            * factor
        )
        return ((grad_keys, grad_values), None)

    result, _ = lax.scan(
        key_advance,
        start_state,
        (split_heads(piece[0], count), split_heads(piece[1], count), log_parts, delta_parts),
    )
    return result


def forward_layer(stream, full, seq_count):
    w_attn, w_mix, w_raise, w_lower, bias_rows, bias_value, bias_raise, gain_rows, shift_rows = full
    total_rows = stream.shape[0]
    rounded = stream.astype(jnp.bfloat16)
    projected = jnp.einsum("td,cde->cte", rounded, w_attn, preferred_element_type=jnp.float32)
    queries = (projected[0] + bias_rows[0].astype(jnp.float32)).astype(jnp.bfloat16)
    keys = projected[1].astype(jnp.bfloat16)
    values = (projected[2] + bias_value.astype(jnp.float32)).astype(jnp.bfloat16)
    seq_shape = (seq_count, total_rows // seq_count, D)
    mixed, logsum = attend_forward(
        queries.reshape(seq_shape), keys.reshape(seq_shape), values.reshape(seq_shape)
    )
    mixed_low = mixed.astype(jnp.bfloat16)
    branch = jnp.dot(mixed_low, w_mix, preferred_element_type=jnp.float32) + bias_rows[1].astype(
        jnp.float32
    )
    normed, scaled_one, inv_one = normalize(
        stream + branch, gain_rows[0].astype(jnp.float32), shift_rows[0].astype(jnp.float32)
    )
    normed_low = normed.astype(jnp.bfloat16)
    upward = jnp.dot(normed_low, w_raise, preferred_element_type=jnp.float32) + bias_raise.astype(
        jnp.float32
    )
    active = exact_gelu(upward).astype(jnp.bfloat16)
    lowered = jnp.dot(active, w_lower, preferred_element_type=jnp.float32) + bias_rows[2].astype(
        jnp.float32
    )
    result, scaled_two, inv_two = normalize(
        normed + lowered, gain_rows[1].astype(jnp.float32), shift_rows[1].astype(jnp.float32)
    )
    states = (
        rounded,
        queries,
        keys,
        values,
        mixed,
        mixed_low,
        logsum,
        scaled_one,
        inv_one,
        normed_low,
        upward,
        active,
        scaled_two,
        inv_two,
    )
    return (result, states)


def backward_layer(grad, full, states, seq_count):
    w_attn, w_mix, w_raise, w_lower, bias_rows, bias_value, bias_raise, gain_rows, shift_rows = full
    (
        rounded,
        queries,
        keys,
        values,
        mixed,
        mixed_low,
        logsum,
        scaled_one,
        inv_one,
        normed_low,
        upward,
        active,
        scaled_two,
        inv_two,
    ) = states
    total_rows = grad.shape[0]
    row_count = total_rows // seq_count
    seq_shape = (seq_count, row_count, D)
    grad_gain_two = jnp.sum(grad * scaled_two, axis=0)
    grad_shift_two = jnp.sum(grad, axis=0)
    grad_resid = norm_back(grad, scaled_two, inv_two, gain_rows[1].astype(jnp.float32))
    grad_lowered = grad_resid.astype(jnp.bfloat16)
    grad_w_lower = jnp.einsum("tf,td->fd", active, grad_lowered, preferred_element_type=jnp.float32)
    grad_active = jnp.einsum("td,fd->tf", grad_lowered, w_lower, preferred_element_type=jnp.float32)
    unused, gelu_back = jax.vjp(exact_gelu, upward)
    grad_upward = gelu_back(grad_active)[0].astype(jnp.bfloat16)
    grad_w_raise = jnp.einsum(
        "td,tf->df", normed_low, grad_upward, preferred_element_type=jnp.float32
    )
    grad_normed = (
        jnp.einsum("tf,df->td", grad_upward, w_raise, preferred_element_type=jnp.float32)
        + grad_resid
    )
    grad_gain_one = jnp.sum(grad_normed * scaled_one, axis=0)
    grad_shift_one = jnp.sum(grad_normed, axis=0)
    grad_inner = norm_back(grad_normed, scaled_one, inv_one, gain_rows[0].astype(jnp.float32))
    grad_branch = grad_inner.astype(jnp.bfloat16)
    grad_w_mix = jnp.einsum("td,te->de", mixed_low, grad_branch, preferred_element_type=jnp.float32)
    grad_mixed = jnp.einsum(
        "te,de->td", grad_branch, w_mix, preferred_element_type=jnp.float32
    ).astype(jnp.bfloat16)
    row_delta = jnp.sum(
        (grad_mixed.astype(jnp.float32) * mixed).reshape(seq_count, row_count, HEADS, HEAD_DIM),
        axis=3,
    ).transpose(0, 2, 1)
    seq_queries = queries.reshape(seq_shape)
    seq_keys = keys.reshape(seq_shape)
    seq_values = values.reshape(seq_shape)
    seq_grad_mixed = grad_mixed.reshape(seq_shape)
    grad_queries = query_fold(seq_queries, seq_grad_mixed, logsum, row_delta, seq_keys, seq_values)
    grad_queries = merge_heads(grad_queries).astype(jnp.bfloat16)
    all_logsum, all_delta = (
        lax.all_gather(logsum, "ctx", axis=2, tiled=True),
        lax.all_gather(row_delta, "ctx", axis=2, tiled=True),
    )
    grad_keys, grad_values = key_fold(
        seq_queries, seq_grad_mixed, seq_keys, seq_values, all_logsum, all_delta
    )
    grad_keys = merge_heads(grad_keys).astype(jnp.bfloat16)
    grad_values = merge_heads(grad_values).astype(jnp.bfloat16)
    grad_project = jnp.stack([grad_queries, grad_keys, grad_values])
    grad_w_attn = jnp.einsum(
        "td,cte->dce", rounded, grad_project, preferred_element_type=jnp.float32
    )
    grad_stream = (
        jnp.einsum("cte,cde->td", grad_project, w_attn, preferred_element_type=jnp.float32)
        + grad_inner
    )
    grad_bias_rows = jnp.stack(
        [
            jnp.sum(grad_queries.astype(jnp.float32), axis=0),
            jnp.sum(grad_branch.astype(jnp.float32), axis=0),
            jnp.sum(grad_lowered.astype(jnp.float32), axis=0),
        ],
        axis=1,
    )
    grad_bias_value = jnp.sum(grad_values.astype(jnp.float32), axis=0)
    grad_bias_raise = jnp.sum(grad_upward.astype(jnp.float32), axis=0)
    local_sums = (
        grad_w_attn,
        grad_w_mix,
        grad_w_raise,
        grad_w_lower,
        grad_bias_rows,
        grad_bias_value,
        grad_bias_raise,
        jnp.stack([grad_gain_one, grad_gain_two], axis=1),
        jnp.stack([grad_shift_one, grad_shift_two], axis=1),
    )
    return (grad_stream, local_sums)


def body(inputs, w_qkv, w_out, w_up, w_down, biases, value_bias, up_bias, gains, shifts, cotangent):
    stacked = (w_qkv, w_out, w_up, w_down, biases, value_bias, up_bias, gains, shifts)
    seq_count = inputs.shape[0]
    stream = inputs.reshape(-1, D).astype(jnp.float32)
    kept_states = []
    for layer in range(LAYERS):
        shards = tuple((array[layer] for array in stacked))
        full = (
            lax.all_gather(shards[0], ("ctx", "fsdp"), axis=1, tiled=True),
            lax.all_gather(shards[1], ("ctx", "fsdp"), axis=0, tiled=True),
            lax.all_gather(shards[2], ("ctx", "fsdp"), axis=0, tiled=True),
            lax.all_gather(shards[3], ("ctx", "fsdp"), axis=0, tiled=True),
            lax.all_gather(shards[4], ("ctx", "fsdp"), axis=1, tiled=True),
            lax.all_gather(shards[5], ("ctx", "fsdp"), axis=0, tiled=True),
            lax.all_gather(shards[6], ("ctx", "fsdp"), axis=0, tiled=True),
            lax.all_gather(shards[7], ("ctx", "fsdp"), axis=1, tiled=True),
            lax.all_gather(shards[8], ("ctx", "fsdp"), axis=1, tiled=True),
        )
        stream, states = forward_layer(stream, full, seq_count)
        kept_states.append(states)
    output = stream.astype(jnp.bfloat16).reshape(inputs.shape)
    grad = cotangent.reshape(-1, D).astype(jnp.float32)
    layer_grads = [None] * LAYERS
    for layer in reversed(range(LAYERS)):
        shards = tuple((array[layer] for array in stacked))
        full = (
            lax.all_gather(shards[0], ("ctx", "fsdp"), axis=1, tiled=True),
            lax.all_gather(shards[1], ("ctx", "fsdp"), axis=0, tiled=True),
            lax.all_gather(shards[2], ("ctx", "fsdp"), axis=0, tiled=True),
            lax.all_gather(shards[3], ("ctx", "fsdp"), axis=0, tiled=True),
            lax.all_gather(shards[4], ("ctx", "fsdp"), axis=1, tiled=True),
            lax.all_gather(shards[5], ("ctx", "fsdp"), axis=0, tiled=True),
            lax.all_gather(shards[6], ("ctx", "fsdp"), axis=0, tiled=True),
            lax.all_gather(shards[7], ("ctx", "fsdp"), axis=1, tiled=True),
            lax.all_gather(shards[8], ("ctx", "fsdp"), axis=1, tiled=True),
        )
        grad, local_sums = backward_layer(grad, full, kept_states[layer], seq_count)
        partial_sums = (
            lax.psum_scatter(local_sums[0], "ctx", scatter_dimension=0, tiled=True),
            lax.psum_scatter(local_sums[1], "ctx", scatter_dimension=0, tiled=True),
            lax.psum_scatter(local_sums[2], "ctx", scatter_dimension=0, tiled=True),
            lax.psum_scatter(local_sums[3], "ctx", scatter_dimension=0, tiled=True),
            lax.psum_scatter(local_sums[4], "ctx", scatter_dimension=0, tiled=True),
            lax.psum_scatter(local_sums[5], "ctx", scatter_dimension=0, tiled=True),
            lax.psum_scatter(local_sums[6], "ctx", scatter_dimension=0, tiled=True),
            lax.psum_scatter(local_sums[7], "ctx", scatter_dimension=0, tiled=True),
            lax.psum_scatter(local_sums[8], "ctx", scatter_dimension=0, tiled=True),
        )
        reduced = (
            lax.psum_scatter(
                partial_sums[0].astype(jnp.bfloat16), "fsdp", scatter_dimension=0, tiled=True
            ).astype(jnp.float32),
            lax.psum_scatter(
                partial_sums[1].astype(jnp.bfloat16), "fsdp", scatter_dimension=0, tiled=True
            ).astype(jnp.float32),
            lax.psum_scatter(
                partial_sums[2].astype(jnp.bfloat16), "fsdp", scatter_dimension=0, tiled=True
            ).astype(jnp.float32),
            lax.psum_scatter(
                partial_sums[3].astype(jnp.bfloat16), "fsdp", scatter_dimension=0, tiled=True
            ).astype(jnp.float32),
            lax.psum_scatter(
                partial_sums[4].astype(jnp.bfloat16), "fsdp", scatter_dimension=0, tiled=True
            ).astype(jnp.float32),
            lax.psum_scatter(
                partial_sums[5].astype(jnp.bfloat16), "fsdp", scatter_dimension=0, tiled=True
            ).astype(jnp.float32),
            lax.psum_scatter(
                partial_sums[6].astype(jnp.bfloat16), "fsdp", scatter_dimension=0, tiled=True
            ).astype(jnp.float32),
            lax.psum_scatter(
                partial_sums[7].astype(jnp.bfloat16), "fsdp", scatter_dimension=0, tiled=True
            ).astype(jnp.float32),
            lax.psum_scatter(
                partial_sums[8].astype(jnp.bfloat16), "fsdp", scatter_dimension=0, tiled=True
            ).astype(jnp.float32),
        )
        layer_grads[layer] = (
            reduced[0].transpose(1, 0, 2),
            reduced[1],
            reduced[2],
            reduced[3],
            reduced[4].T,
            reduced[5],
            reduced[6],
            reduced[7].T,
            reduced[8].T,
        )
    grad_inputs = grad.astype(jnp.bfloat16).reshape(inputs.shape)
    return (
        output,
        grad_inputs,
        jnp.stack([member[0] for member in layer_grads]),
        jnp.stack([member[1] for member in layer_grads]),
        jnp.stack([member[2] for member in layer_grads]),
        jnp.stack([member[3] for member in layer_grads]),
        jnp.stack([member[4] for member in layer_grads]),
        jnp.stack([member[5] for member in layer_grads]),
        jnp.stack([member[6] for member in layer_grads]),
        jnp.stack([member[7] for member in layer_grads]),
        jnp.stack([member[8] for member in layer_grads]),
    )


def one_group_per_sequence(mesh, seqs):
    return mesh.shape["fsdp"] == 4 and mesh.shape["ctx"] == seqs


def solution(mesh):
    def run(*arrays):
        seqs = arrays[0].shape[0]
        chosen = grouped(mesh.shape["ctx"] // 2, 2) if one_group_per_sequence(mesh, seqs) else body
        return on_devices(mesh, chosen)(*arrays)

    return run


def on_devices(mesh, chosen):
    return jax.shard_map(
        chosen,
        mesh=mesh,
        in_specs=(
            P("fsdp", "ctx", None),
            P(None, None, ("ctx", "fsdp"), None),
            P(None, ("ctx", "fsdp"), None),
            P(None, ("ctx", "fsdp"), None),
            P(None, ("ctx", "fsdp"), None),
            P(None, None, ("ctx", "fsdp")),
            P(None, ("ctx", "fsdp")),
            P(None, ("ctx", "fsdp")),
            P(None, None, ("ctx", "fsdp")),
            P(None, None, ("ctx", "fsdp")),
            P("fsdp", "ctx", None),
        ),
        out_specs=(
            P("fsdp", "ctx", None),
            P("fsdp", "ctx", None),
            P(None, None, ("ctx", "fsdp"), None),
            P(None, ("ctx", "fsdp"), None),
            P(None, ("ctx", "fsdp"), None),
            P(None, ("ctx", "fsdp"), None),
            P(None, None, ("ctx", "fsdp")),
            P(None, ("ctx", "fsdp")),
            P(None, ("ctx", "fsdp")),
            P(None, None, ("ctx", "fsdp")),
            P(None, None, ("ctx", "fsdp")),
        ),
        check_vma=False,
    )
```

profile of v0, /device:TPU:1, one launch (start us, length us, event | category | flops | bytes accessed | tf_op | source)
XLA Modules:
  0.0 221.5 jit_solution(1901436794559660180)
XLA Ops:
  0.6 1.3 copy.22.refs_5_
  1.9 215.4 %shard_map.194 = (bf16[2,64,768]{2,1,0:T(8,128)(2,1)}, bf16[2,64,768]{2,1,0:T(8,128)(2,1)}, f32[2,3,24,768]{3,2,1,0:T(8,128)}, f32[2,24,768]{2,1,0:T(8,128)}, f3...) custom-call(bf16[2,64,768]{2,1,0:T(8,128)(2,1)} %refs_0_.1, ...), custom_call_target="tpu_custom_call" | custom-call | tf_op jit(solution)/shard_map/pallas_call | solution.py:1349
  217.3 3.0 %shard_map.195 = (bf16[2,64,768]{2,1,0:T(8,128)(2,1)}, bf16[2,64,768]{2,1,0:T(8,128)(2,1)}, f32[2,3,24,768]{3,2,1,0:T(8,128)}, f32[2,24,768]{2,1,0:T(8,128)}, f3...) custom-call(bf16[2,64,768]{2,1,0:T(8,128)(2,1)} %get-tuple-element.2, ...), custom_call_target="tpu_custom_call" | custom-call | tf_op jit(solution)/shard_map/pallas_call | solution.py:1359
  220.3 0.0 copy-start
  220.3 0.7 copy-done
  221.0 0.6 copy.23
Async XLA Ops:
  220.3 0.7 copy-start
where the time goes:
time: 222 us
  Pallas kernels  218 us (98%)
  local copies, waits for them, and re-layouts  2.52 us (1%)
    pallas_call x1, Pallas kernels, run(): pl.pallas_call(functools.partial(group_kernel, layout, nz), out_shape=tup...  215 us

commit v1 on v0

--- a/solution.py
+++ b/solution.py
@@ -141,10 +141,10 @@
         inx_r=dma((2, 2)),
         ins_s=dma((1,)),
         ins_r=dma((1,)),
-        gz_s=dma((8, nz)),
-        gz_r=dma((8, nz)),
-        gy_s=dma((8, nz)),
-        gy_r=dma((8, nz)),
+        gz_s=dma((10, nz)),
+        gz_r=dma((10, nz)),
+        gy_s=dma((10, nz)),
+        gy_r=dma((10, nz)),
         sib_s=dma((2, half // PIECE)),
         sib_r=dma((2, half // PIECE)),
         x_s=dma((2, half // PIECE)),
@@ -262,7 +262,8 @@
         S.sf[...] = jnp.zeros_like(S.sf)
         for layer in range(LAYERS):
             base = 8 * layer
-            S.sf[base : base + 3, 0:d_rows] = biases[layer].astype(F32)
+            for kind in range(3):
+                S.sf[base + kind : base + kind + 1, 0:d_rows] = biases[kind, layer : layer + 1].astype(F32)
             S.sf[base + 3 : base + 4, 0:d_rows] = value_bias[layer : layer + 1].astype(F32)
             S.sf[base + 4 : base + 6, 0:d_rows] = gains[layer].astype(F32)
             S.sf[base + 6 : base + 8, 0:d_rows] = shifts[layer].astype(F32)
@@ -354,7 +355,6 @@
         def _():
             perm_copy.start()
 
-    start_perm()
     for r in (1, 2, 0):
         stage_copy(2, r).start()
     S.smg[z, y, m] = s_in[...]
@@ -383,8 +383,8 @@
     def at_z(z_at):
         return dev(z_at, x, y, c)
 
-    LAST = -1
-    DIRECT = 0
+    half_rows = f_rows // 2
+    upper, lower = pl.ds(0, half_rows), pl.ds(half_rows, half_rows)
 
     def slab(cls, z_at, y_at):
         return (
@@ -395,58 +395,48 @@
             lambda: S.wd.at[0, z_at, y_at],
             lambda: S.wq.at[1, z_at, :, y_at],
             lambda: S.wu.at[1, z_at, :, y_at],
-            lambda: S.wd.at[1, z_at, y_at],
+            lambda: S.wd.at[1, z_at, y_at, upper],
+            lambda: S.wd.at[1, z_at, y_at, lower],
         )[cls]()
 
+    def y_first(cls):
+        return cls >= 8
+
     def z_copy(cls, n, z_at, to):
-        spot = S.wd.at[1, z_at] if cls == LAST else slab(cls, z_at, y)
+        spot = S.wd.at[1, z_at, :, lower] if y_first(cls) else slab(cls, z_at, y)
         return rcopy(spot, spot, S.gz_s.at[cls, n], S.gz_r.at[cls, z_at], at_z(to))
 
     def y_copy(cls, z_at):
         spot = slab(cls, z_at, y)
         return rcopy(spot, spot, S.gy_s.at[cls, z_at], S.gy_r.at[cls, z_at], across)
 
-    def gather_direct(cls):
-        z_copy(cls, 0, z, buddy).start()
-        z_copy(cls, 1, z, far_in).start()
-        if cls < DIRECT:
-            z_copy(cls, 2, z, far_out).start()
+    def y_wait(cls, t):
+        spot = slab(cls, t, 1 - y)
+        rcopy(spot, spot, S.gy_s.at[cls, t], S.gy_r.at[cls, t], across).wait_recv()
 
     def gather_start(cls):
-        if cls != LAST:
-            gather_direct(cls)
+        if not y_first(cls):
+            z_copy(cls, 0, z, buddy).start()
+            z_copy(cls, 1, z, far_in).start()
         y_copy(cls, z).start()
 
     def gather_cross(cls):
-        if cls != LAST:
-            return
-        spot = slab(cls, z, 1 - y)
-        rcopy(spot, spot, S.gy_s.at[cls, z], S.gy_r.at[cls, z], across).wait_recv()
-        gather_direct(cls)
+        y_wait(cls, z)
+        for n, to in enumerate((buddy, far_in, far_out)):
+            z_copy(cls, n, z, to).start()
 
     def gather_take(cls, z_at, relay):
         z_copy(cls, 0, z_at, buddy).wait_recv()
         if relay is not None:
             z_copy(cls, relay, z_at, near_out).start()
-        if cls != LAST:
-            y_copy(cls, z_at).start()
+        y_copy(cls, z_at).start()
 
     def gather_relay(cls):
         gather_take(cls, buddy, None)
-        if cls < DIRECT:
-            gather_take(cls, far_in, None)
-            gather_take(cls, far_out, None)
-            return
 
         @pl.when(inner)
         def _():
             gather_take(cls, far_in, 2)
-
-        gather_relay_far(cls)
-
-    def gather_relay_far(cls):
-        @pl.when(inner)
-        def _():
             gather_take(cls, far_out, 3)
 
     def gather_end(cls):
@@ -456,37 +446,32 @@
             gather_take(cls, far_out, None)
 
     def gather_wait(cls):
-        if cls == LAST:
-            spot = S.wd.at[1, z]
+        if y_first(cls):
+            for t in (buddy, far_in, far_out):
+                z_copy(cls, 0, t, buddy).wait_recv()
             return
 
-        def one(t):
-            spot = slab(cls, t, 1 - y)
-            rcopy(spot, spot, S.gy_s.at[cls, t], S.gy_r.at[cls, t], across).wait_recv()
-
         for t in (z, buddy, far_in, far_out):
-            one(t)
+            y_wait(cls, t)
 
     def gather_drain(cls):
         z_copy(cls, 0, z, buddy).wait_send()
         z_copy(cls, 1, z, far_in).wait_send()
-        if cls < DIRECT:
+        if y_first(cls):
             z_copy(cls, 2, z, far_out).wait_send()
-        else:
-
-            @pl.when(inner)
-            def _():
-                z_copy(cls, 2, far_in, near_out).wait_send()
-                z_copy(cls, 3, far_out, near_out).wait_send()
+            y_copy(cls, z).wait_send()
+            return
+
+        @pl.when(inner)
+        def _():
+            z_copy(cls, 2, far_in, near_out).wait_send()
+            z_copy(cls, 3, far_out, near_out).wait_send()
 
         def one(t, carry):
             y_copy(cls, t).wait_send()
             return carry
 
-        if cls == LAST:
-            one(z, 0)
-        else:
-            lax.fori_loop(0, nz, one, 0)
+        lax.fori_loop(0, nz, one, 0)
 
     for r in range(3):
         stage_wait(1, r)
@@ -513,6 +498,7 @@
     theirs = half * (1 - c)
     scatter_in_wait(0, inp, first, mine + block * x)
     swap_start(0, first, mine)
+    start_perm()
     for r in range(3):
         stage_wait(2, r)
     join(S.us, S.wu)
@@ -795,9 +781,9 @@
     gather_wait(1)
     for i in range(pieces):
         project(0, i)
-    gather_start(4)
     gather_end(2)
     gather_relay(3)
+    gather_start(4)
     out_weights()
     pipeline(
         (lambda i: attend(0, i), lambda i: part_pass(0, i)),
@@ -806,6 +792,7 @@
     pipeline((lambda i: after_attention(0, i),))
     part_drain(0)
     gather_start(6)
+    gather_start(8)
     gather_end(4)
     gather_wait(3)
     pipeline((lambda i: raise_part(0, i),))
@@ -817,10 +804,11 @@
     pipeline((lambda i: lower_part(0, i), lambda i: part_pass(1, i)))
     swap_start(1, S.ct, 0)
     gather_relay(6)
+    gather_cross(8)
     gather_wait(5)
     pipeline(
         (lambda i: after_lower(0, i), lambda i: next_project(1, i)),
-        {0: [lambda: gather_end(6)], 3: [lambda: gather_cross(7)]},
+        {0: [lambda: gather_end(6)]},
     )
     part_drain(1)
     pipeline(
@@ -835,7 +823,7 @@
             lambda i: lower_part(1, i),
             lambda i: part_pass(1, i),
         ),
-        {1: [lambda: gather_wait(7)]},
+        {1: [lambda: gather_wait(7), lambda: gather_wait(8)]},
     )
     part_drain(0)
     swap_wait(1, S.ct, 0)
@@ -1183,14 +1171,15 @@
         pick = jnp.where((col == d_rows * d + lane) & narrow, 1.0, 0.0)
         both = S.sga[layer, 2 * x] + S.sga[layer, 2 * x + 1]
         found = dot_exact(both, pick)[:, 0:d_rows]
-        g_biases[layer, 1:3, :] = found[0:2]
+        g_biases[1, layer : layer + 1, :] = found[0:1]
+        g_biases[2, layer : layer + 1, :] = found[1:2]
         g_gains[layer] = found[2:4]
         g_shifts[layer] = found[4:6]
         dim, is_query, is_value = packed_lanes((D, 128), 0)
         hit = (dim == d_rows * (d - 8 * z) + lane) & narrow
         attn = S.sga[layer, z]
         found = dot_exact(attn, jnp.where(hit & is_query, 1.0, 0.0))
-        g_biases[layer, 0:1, :] = found[7:8, 0:d_rows]
+        g_biases[0, layer : layer + 1, :] = found[7:8, 0:d_rows]
         found = dot_exact(attn, jnp.where(hit & is_value, 1.0, 0.0))
         g_value[layer : layer + 1, :] = found[7:8, 0:d_rows]
         pick = jnp.where((col == f_rows * (2 * z + y) + lane) & (lane < f_rows), 1.0, 0.0)
@@ -1317,7 +1306,7 @@
 
     spot = first.at[pl.ds(mine, half)]
     rcopy(spot, spot, S.ins_s.at[0], S.ins_r.at[0], sibling).wait_send()
-    for cls in range(8):
+    for cls in range(9):
         gather_drain(cls)
     scatter_out_wait(0, S.back.at[0], out)
     scatter_out_wait(1, S.back.at[1], gin)
@@ -1343,7 +1332,7 @@
         half = rows // 2
         layout = scratch_layout(nz, ny, rows, half, d_rows, f_rows)
         vmem = pl.BlockSpec(memory_space=pltpu.VMEM)
-        weights = (w_qkv, w_out, w_up, w_down, biases, value_bias, up_bias, gains, shifts)
+        weights = (w_qkv, w_out, w_up, w_down, biases.transpose(1, 0, 2), value_bias, up_bias, gains, shifts)
         shapes = [jax.ShapeDtypeStruct(inputs.shape, BF)] * 2
         shapes += [jax.ShapeDtypeStruct(array.shape, F32) for array in weights]
         results = pl.pallas_call(
@@ -1356,12 +1345,13 @@
                 collective_id=0, has_side_effects=True, vmem_limit_bytes=KERNEL_VMEM
             ),
         )(inputs, *weights, cotangent)
-        return pl.pallas_call(
+        handed = pl.pallas_call(
             hand_over,
             out_shape=tuple(shapes),
             in_specs=[vmem] * 11,
             out_specs=[vmem] * 11,
         )(*results)
+        return (*handed[:6], handed[6].transpose(1, 0, 2), *handed[7:])
 
     return run
 

time: 222 us -> 214 us (0.964)
  Pallas kernels: 218 us -> 213 us
  local copies, waits for them, and re-layouts: 2.52 us -> 0 us
    pallas_call x1, Pallas kernels: 215 us -> 210 us  [run(): pl.pallas_call(functools.partial(group_kernel, layout, nz), out_shape=tup...]
where the time goes in v1:
time: 214 us
  Pallas kernels  213 us (100%)
    pallas_call x1, Pallas kernels, run(): pl.pallas_call(functools.partial(group_kernel, layout, nz), out_shape=tup...  210 us

profile of v1, /device:TPU:1, one launch (start us, length us, event | category | flops | bytes accessed | tf_op | source)
XLA Modules:
  0.0 214.0 jit_solution(13281776019422055509)
XLA Ops:
  0.6 210.1 %shard_map.194 = (bf16[2,64,768]{2,1,0:T(8,128)(2,1)}, bf16[2,64,768]{2,1,0:T(8,128)(2,1)}, f32[2,3,24,768]{3,2,1,0:T(8,128)}, f32[2,24,768]{2,1,0:T(8,128)}, f3...) custom-call(bf16[2,64,768]{2,1,0:T(8,128)(2,1)} %refs_0_.1, ...), custom_call_target="tpu_custom_call" | custom-call | tf_op jit(solution)/shard_map/pallas_call | solution.py:1338
  210.8 3.0 %shard_map.195 = (bf16[2,64,768]{2,1,0:T(8,128)(2,1)}, bf16[2,64,768]{2,1,0:T(8,128)(2,1)}, f32[2,3,24,768]{3,2,1,0:T(8,128)}, f32[2,24,768]{2,1,0:T(8,128)}, f3...) custom-call(bf16[2,64,768]{2,1,0:T(8,128)(2,1)} %get-tuple-element.3, ...), custom_call_target="tpu_custom_call" | custom-call | tf_op jit(solution)/shard_map/pallas_call | solution.py:1348
